TPU v7x, 32 devices: a whole 2x2x4 slice. The times are simulated.
32 devices in a mesh: seq: 8 (over z, y), head: 4 (over x, core).
Axes of the slice: x: 2, y: 2, z: 4, core: 2. Of those that a mesh axis runs over, the one named last changes fastest.
Arguments:
- tokens: bfloat16 [16384, 2048], P(('seq', 'head')), may hold values from -60 to 60
- query_index: int32 [1024], replicated, may hold values from 0 to 16383, as said below
- key_index: int32 [1024], replicated, may hold values from 0 to 16383, as said below
- light_query: bfloat16 [2048, 256], replicated, may hold values from -0.1875 to 0.1875
- light_key: bfloat16 [2048, 256], replicated, may hold values from -0.1875 to 0.1875
- light_value: bfloat16 [2048, 256], replicated, may hold values from -0.125 to 0.125
- light_out: bfloat16 [256, 2048], replicated, may hold values from -0.375 to 0.375
- heavy_query: bfloat16 [2048, 1024], P(None, 'head'), may hold values from -0.1875 to 0.1875
- heavy_key: bfloat16 [2048, 1024], P(None, 'head'), may hold values from -0.1875 to 0.1875
- heavy_value: bfloat16 [2048, 1024], P(None, 'head'), may hold values from -0.125 to 0.125
- heavy_out: bfloat16 [1024, 2048], P('head'), may hold values from -0.1875 to 0.1875
Outputs:
- layer_out: bfloat16 [16384, 2048], P(('seq', 'head'))
Inputs may be any that keep to these rules, and one draw needn't show every extreme that they name: `query_index`: ascending and distinct token positions; at most 512 of them lie in one block of 2048 tokens starting at a multiple of 2048, and some block holds exactly 512. `key_index`: ascending and distinct token positions; at most 192 of them lie in one block of 2048 tokens starting at a multiple of 2048, and some block holds exactly 192.
All inputs are finite; a program needn't handle non-finite values.
Results may differ from a plain program's by a relative error of at most 0.02.
Values may be sent and summed in bfloat16 or wider, within the bound.
A program may use at most 128 MiB of HBM per device.

v0:
```python
import jax
import jax.numpy as jnp
from jax import lax
from jax.sharding import PartitionSpec as P

HDIM = 64
LHEADS = 4
RADIUS = 127


floor_score = -1e30


def padded_2(block, sides, width):
    for axis, dim in sides:
        count = lax.axis_size(axis)
        forward = [(i, i + 1) for i in range(count - 1)]
        backward = [(target, source) for source, target in forward]
        low = lax.ppermute(
            lax.slice_in_dim(block, block.shape[dim] - width, None, axis=dim), axis, forward
        )
        high = lax.ppermute(lax.slice_in_dim(block, 0, width, axis=dim), axis, backward)
        block = jnp.concatenate([low, block, high], axis=dim)
    return block


def partial_stats(query_rows, key_rows, value_rows, allowed, head_count):
    row_count = query_rows.shape[0]
    key_count = key_rows.shape[0]
    head_dim = query_rows.shape[1] // head_count
    query_split = query_rows.reshape(row_count, head_count, head_dim)
    key_split = key_rows.reshape(key_count, head_count, head_dim)
    value_split = value_rows.reshape(key_count, head_count, head_dim)
    scores = jnp.einsum(
        "qhd,khd->hqk", query_split, key_split, preferred_element_type=jnp.float32
    ) * head_dim ** (-0.5)
    scores = jnp.where(allowed[None], scores, floor_score)
    row_peak = jnp.max(scores, axis=2)
    weights = jnp.where(allowed[None], jnp.exp(scores - row_peak[:, :, None]), 0.0)
    row_total = jnp.sum(weights, axis=2)
    blended = jnp.einsum(
        "hqk,khd->qhd",
        weights.astype(jnp.bfloat16),
        value_split,
        preferred_element_type=jnp.float32,
    )
    return (blended.reshape(row_count, head_count * head_dim), row_peak.T, row_total.T)


def scale_heads(acc_rows, factor):
    row_count = acc_rows.shape[0]
    head_count = factor.shape[1]
    width = acc_rows.shape[1]
    return (
        acc_rows.reshape(row_count, head_count, width // head_count) * factor[:, :, None]
    ).reshape(row_count, width)


def normalize(acc_rows, total_rows):
    return scale_heads(acc_rows, 1.0 / total_rows).astype(jnp.bfloat16)


def shards(
    tokens,
    query_index,
    key_index,
    light_query,
    light_key,
    light_value,
    light_out,
    heavy_query,
    heavy_key,
    heavy_value,
    heavy_out,
):
    row_count = tokens.shape[0]
    model_width = tokens.shape[1]
    group_size = lax.axis_size("head")
    seq_count = lax.axis_size("seq")
    block_len = row_count * group_size
    seq_rank = lax.axis_index("seq")
    head_rank = lax.axis_index("head")
    my_first = (seq_rank * group_size + head_rank) * row_count
    total_len = block_len * seq_count
    query_cap = block_len // 4
    key_cap = 3 * block_len // 32
    query_total = query_index.shape[0]
    key_total = key_index.shape[0]
    light_width = light_query.shape[1]
    heavy_width = heavy_query.shape[1]
    heads_here = heavy_width // HDIM
    light_rows = jnp.dot(tokens, light_query, preferred_element_type=jnp.float32).astype(
        jnp.bfloat16
    )
    light_pair = jnp.concatenate(
        [
            jnp.dot(tokens, light_key, preferred_element_type=jnp.float32),
            jnp.dot(tokens, light_value, preferred_element_type=jnp.float32),
        ],
        axis=1,
    ).astype(jnp.bfloat16)
    padded = padded_2(light_pair, ((("seq", "head"), 0),), RADIUS)
    query_pos = my_first + jnp.arange(row_count, dtype=jnp.int32)
    key_pos = my_first - RADIUS + jnp.arange(row_count + 2 * RADIUS, dtype=jnp.int32)
    allowed = (
        (jnp.abs(query_pos[:, None] - key_pos[None, :]) <= RADIUS)
        & (key_pos[None, :] >= 0)
        & (key_pos[None, :] < total_len)
    )
    light_acc, light_peak, light_total = partial_stats(
        light_rows, padded[:, :light_width], padded[:, light_width:], allowed, LHEADS
    )
    light_mixed = normalize(light_acc, light_total)
    light_term = jnp.dot(light_mixed, light_out, preferred_element_type=jnp.float32)
    block_starts = jnp.arange(seq_count, dtype=jnp.int32) * block_len
    query_starts = jnp.sum((query_index[None, :] < block_starts[:, None]).astype(jnp.int32), axis=1)
    key_starts = jnp.sum((key_index[None, :] < block_starts[:, None]).astype(jnp.int32), axis=1)
    query_counts = (
        jnp.concatenate([query_starts[1:], jnp.full((1,), query_total, jnp.int32)]) - query_starts
    )
    key_counts = (
        jnp.concatenate([key_starts[1:], jnp.full((1,), key_total, jnp.int32)]) - key_starts
    )
    query_first = query_starts[seq_rank]
    key_first = key_starts[seq_rank]
    query_slots = jnp.arange(query_cap, dtype=jnp.int32)
    key_slots = jnp.arange(key_cap, dtype=jnp.int32)
    query_valid = query_slots < query_counts[seq_rank]
    key_valid = key_slots < key_counts[seq_rank]
    query_padded = jnp.concatenate([query_index, jnp.zeros((query_cap,), jnp.int32)])
    key_padded = jnp.concatenate([key_index, jnp.zeros((key_cap,), jnp.int32)])
    query_run = lax.dynamic_slice_in_dim(query_padded, query_first, query_cap, 0)
    key_run = lax.dynamic_slice_in_dim(key_padded, key_first, key_cap, 0)
    query_place = jnp.where(query_valid, query_run - seq_rank * block_len, 0)
    key_place = jnp.where(key_valid, key_run - seq_rank * block_len, 0)
    block_rows = lax.all_gather(tokens, "head", axis=0, tiled=True)
    query_tokens = block_rows[query_place]
    key_tokens = block_rows[key_place]
    routed_q = jnp.where(
        query_valid[:, None],
        jnp.dot(query_tokens, heavy_query, preferred_element_type=jnp.float32),
        0.0,
    ).astype(jnp.bfloat16)
    routed_pair = jnp.concatenate(
        [
            jnp.dot(key_tokens, heavy_key, preferred_element_type=jnp.float32),
            jnp.dot(key_tokens, heavy_value, preferred_element_type=jnp.float32),
        ],
        axis=1,
    ).astype(jnp.bfloat16)
    share_len = query_total // seq_count
    dense = jnp.zeros((query_total + query_cap, heavy_width), jnp.bfloat16)
    dense = lax.dynamic_update_slice_in_dim(dense, routed_q, query_first, 0)[:query_total]
    spread = lax.all_to_all(dense, "seq", split_axis=0, concat_axis=0, tiled=True)
    balanced = jnp.sum(
        spread.reshape(seq_count, share_len, heavy_width).astype(jnp.float32), axis=0
    ).astype(jnp.bfloat16)
    every_query = lax.all_gather(balanced, "seq", axis=0, tiled=True)
    part_acc, part_peak, part_total = partial_stats(
        every_query,
        routed_pair[:, :heavy_width],
        routed_pair[:, heavy_width:],
        key_valid[None, :],
        heads_here,
    )
    acc_in, peak_in, total_in = (
        lax.all_to_all(part_acc, "seq", split_axis=0, concat_axis=0, tiled=True),
        lax.all_to_all(part_peak, "seq", split_axis=0, concat_axis=0, tiled=True),
        lax.all_to_all(part_total, "seq", split_axis=0, concat_axis=0, tiled=True),
    )
    acc_in = acc_in.reshape(seq_count, share_len, heads_here, HDIM)
    peak_in = peak_in.reshape(seq_count, share_len, heads_here)
    total_in = total_in.reshape(seq_count, share_len, heads_here)
    joint_peak = jnp.max(peak_in, axis=0)
    scale_in = jnp.exp(peak_in - joint_peak[None])
    joint_total = jnp.sum(total_in * scale_in, axis=0)
    joint_acc = jnp.sum(acc_in * scale_in[:, :, :, None], axis=0).reshape(share_len, heavy_width)
    answer = normalize(joint_acc, joint_total)
    owner_block = (
        lax.dynamic_slice_in_dim(query_index, seq_rank * share_len, share_len, 0) // block_len
    )
    outgoing = jnp.where(
        owner_block[None, :, None] == jnp.arange(seq_count, dtype=jnp.int32)[:, None, None],
        answer[None],
        jnp.zeros((), jnp.bfloat16),
    )
    returned = lax.all_to_all(
        outgoing.reshape(seq_count * share_len, heavy_width),
        "seq",
        split_axis=0,
        concat_axis=0,
        tiled=True,
    )
    padded_back = jnp.concatenate(
        [returned, jnp.zeros((query_cap, heavy_width), jnp.bfloat16)], axis=0
    )
    owner_mixed = lax.dynamic_slice_in_dim(padded_back, query_first, query_cap, 0)
    head_term = jnp.where(
        query_valid[:, None],
        jnp.dot(owner_mixed, heavy_out, preferred_element_type=jnp.float32),
        0.0,
    )
    summed = lax.psum(head_term.astype(jnp.bfloat16), "head").astype(jnp.float32)
    local_row = query_place - head_rank * row_count
    local_row = jnp.where(
        query_valid & (local_row >= 0) & (local_row < row_count), local_row, row_count
    )
    heavy_term = (
        jnp.zeros((row_count, model_width), jnp.float32).at[local_row].add(summed, mode="drop")
    )
    return (light_term + heavy_term).astype(jnp.bfloat16)


def solution(mesh):
    placed = (
        P(("seq", "head"), None),
        P(),
        P(),
        P(),
        P(),
        P(),
        P(),
        P(None, "head"),
        P(None, "head"),
        P(None, "head"),
        P("head", None),
    )
    return jax.shard_map(
        shards, mesh=mesh, in_specs=placed, out_specs=P(("seq", "head"), None), check_vma=False
    )
```

profile of v0, /device:TPU:0, one launch (start us, length us, event | category | flops | bytes accessed | tf_op | source)
XLA Modules:
  0.0 274.2 jit_solution(11924041511517521918)
XLA Ops:
  14.3 55.7 %all-gather.2.cloned.1.call-done = bf16[2048,2048]{1,0:T(8,128)(2,1)} async-done(((bf16[512,2048]{1,0:T(8,128)(2,1)}), bf16[2048,2048]{1,0:T(8,128)(2,1)}) %all-gather.2.cloned.1.call-update) | async-done | bytes 8388624 | tf_op jit(solution)/shard_map/all_gather | solution.py:136
  69.9 8.9 %gather_fusion.1 = bf16[512,2048]{1,0:T(8,128)(2,1)S(1)} fusion(bf16[2048,2048]{1,0:T(8,128)(2,1)} %all-gather.2.cloned.1.call-done, s32[1024]{0:T(1024)S(1)} %pad_clamp_fusion), kind=kCustom, calls=%fused_computation.1 | custom fusion | bytes 4196352 | tf_op jit(solution)/shard_map/gather | solution.py:137
  83.6 5.3 %all-to-all-start = ((bf16[8,128,256]{2,1,0:T(8,128)(2,1)}), bf16[8,128,256]{2,1,0:T(8,128)(2,1)S(1)}, u32[]{:S(2)}, u32[]{:S(2)}) async-start(bf16[8,128,256]{2,1,0:T(8,128)(2,1)} %bitcast.11), calls=%async_computation | async-start | bytes 1048576 | tf_op jit(solution)/shard_map/all_to_all | solution.py:154
  93.1 6.5 %gather_fusion = bf16[192,2048]{1,0:T(8,128)(2,1)S(1)} fusion(bf16[2048,2048]{1,0:T(8,128)(2,1)} %all-gather.2.cloned.1.call-done, s32[1024]{0:T(1024)S(1)} %pad_clamp_fusion.1), kind=kCustom, calls=%fused_computation | custom fusion | bytes 1573632 | tf_op jit(solution)/shard_map/gather | solution.py:138
  100.0 3.7 %all-to-all-done = bf16[8,128,256]{2,1,0:T(8,128)(2,1)S(1)} async-done(((bf16[8,128,256]{2,1,0:T(8,128)(2,1)}), bf16[8,128,256]{2,1,0:T(8,128)(2,1)S(1)}, u32[]{:S(2)}, u32[]{:S(2)}) %all-to-all-start) | async-done | bytes 524320 | tf_op jit(solution)/shard_map/all_to_all | solution.py:154
  103.8 31.3 %all_gather.7 = bf16[1024,256]{1,0:T(8,128)(2,1)S(1)} all-gather(bf16[128,256]{1,0:T(8,128)(2,1)S(1)} %reduce_sum.69), channel_id=1, replica_groups=mesh['seq'=8,'head'=4] {'seq'}, dimensions={0}, use_global_device_ids=true | all-gather | bytes 589824 | tf_op jit(solution)/shard_map/all_gather | solution.py:158
  140.4 3.8 %all-to-all-start.3 = ((f32[8,128,4]{1,2,0:T(4,128)}), f32[8,128,4]{1,2,0:T(4,128)S(1)}, u32[]{:S(2)}, u32[]{:S(2)}) async-start(f32[8,128,4]{1,2,0:T(4,128)} %bitcast.19), calls=%async_computation.3 | async-start | bytes 32768 | tf_op jit(solution)/shard_map/all_to_all | solution.py:169
  144.7 6.1 %all-to-all-done.3 = f32[8,128,4]{1,2,0:T(4,128)S(1)} async-done(((f32[8,128,4]{1,2,0:T(4,128)}), f32[8,128,4]{1,2,0:T(4,128)S(1)}, u32[]{:S(2)}, u32[]{:S(2)}) %all-to-all-start.3) | async-done | bytes 16416 | tf_op jit(solution)/shard_map/all_to_all | solution.py:169
  150.8 3.3 %all-to-all-start.2 = ((f32[8,128,4]{1,2,0:T(4,128)}), f32[8,128,4]{1,2,0:T(4,128)S(1)}, u32[]{:S(2)}, u32[]{:S(2)}) async-start(f32[8,128,4]{1,2,0:T(4,128)} %bitcast.16), calls=%async_computation.2 | async-start | bytes 32768 | tf_op jit(solution)/shard_map/all_to_all | solution.py:168
  154.1 2.8 %fusion.12 = f32[4,64,1024]{2,1,0:T(8,128)S(1)} fusion(bf16[192,4,64]{0,2,1:T(8,128)(2,1)S(1)} %bitcast.73, f32[4,1024,192]{1,2,0:T(8,128)} %copy-done.1, f32[4,1024]{1,0:T(4,128)} %get-tuple-element.17, pred[192]{0:T(512)(128)(4,1)S(1)} %iota_compare_fusion.2), kind=kOutput, calls=%fused_computation.21 | convolution fusion | flops 104595456 | bytes 4309184 | tf_op jit(solution)/shard_map/hqk,khd->qhd/dot_general | solution.py:41
  158.2 2.4 all-to-all-done.2
  160.7 3.6 %all-to-all-start.1 = ((f32[8,128,256]{1,2,0:T(8,128)}), f32[8,128,256]{1,2,0:T(8,128)S(1)}, u32[]{:S(2)}, u32[]{:S(2)}) async-start(f32[8,128,256]{1,2,0:T(8,128)} %copy.25), calls=%async_computation.1 | async-start | bytes 2097152 | tf_op jit(solution)/shard_map/all_to_all | solution.py:167
  164.3 2.8 %convolution_convert_fusion.1 = bf16[512,256]{0,1:T(8,128)(2,1)S(1)} fusion(bf16[512,2048]{1,0:T(8,128)(2,1)} %param.11, bf16[2048,256]{1,0:T(8,128)(2,1)} %param.16), kind=kOutput, calls=%fused_computation.31 | convolution fusion | flops 537001984 | bytes 3407872 | tf_op jit(solution)/shard_map/dot_general | solution.py:98
  172.6 9.9 %all-to-all-done.1 = f32[8,128,256]{1,2,0:T(8,128)S(1)} async-done(((f32[8,128,256]{1,2,0:T(8,128)}), f32[8,128,256]{1,2,0:T(8,128)S(1)}, u32[]{:S(2)}, u32[]{:S(2)}) %all-to-all-start.1) | async-done | bytes 1048608 | tf_op jit(solution)/shard_map/all_to_all | solution.py:167
  183.7 3.6 %all-to-all-start.4 = ((bf16[8,128,256]{2,1,0:T(8,128)(2,1)}), bf16[8,128,256]{2,1,0:T(8,128)(2,1)S(1)}, u32[]{:S(2)}, u32[]{:S(2)}) async-start(bf16[8,128,256]{2,1,0:T(8,128)(2,1)} %broadcast_select_fusion), calls=%async_computation.4 | async-start | bytes 1048576 | tf_op jit(solution)/shard_map/all_to_all | solution.py:187
  187.6 3.3 %convolution_convert_fusion = bf16[512,256]{0,1:T(8,128)(2,1)} fusion(bf16[512,2048]{1,0:T(8,128)(2,1)} %param.11, bf16[2048,256]{1,0:T(8,128)(2,1)} %param.14), kind=kOutput, calls=%fused_computation.30 | convolution fusion | flops 537001984 | bytes 3407872 | tf_op jit(solution)/shard_map/dot_general | solution.py:92
  191.9 6.3 %all-to-all-done.4 = bf16[8,128,256]{2,1,0:T(8,128)(2,1)S(1)} async-done(((bf16[8,128,256]{2,1,0:T(8,128)(2,1)}), bf16[8,128,256]{2,1,0:T(8,128)(2,1)S(1)}, u32[]{:S(2)}, u32[]{:S(2)}) %all-to-all-start.4) | async-done | bytes 524320 | tf_op jit(solution)/shard_map/all_to_all | solution.py:187
  198.2 2.8 %select_convert_fusion = bf16[512,2048]{1,0:T(8,128)(2,1)} fusion(bf16[256,2048]{1,0:T(8,128)(2,1)S(1)} %copy-done, pred[512]{0:T(512)(128)(4,1)} %copy-done.8, s32[]{:T(128)S(6)} %select_n.73, bf16[1024,256]{1,0:T(8,128)(2,1)S(1)} %bitcast.71), kind=kOutput, calls=%fused_computation.9 | convolution fusion | flops 538968064 | bytes 3670532 | tf_op jit(solution)/shard_map/dot_general | solution.py:200
  201.1 4.6 %fusion.47 = (f32[4,512]{1,0:T(4,128)S(1)}, bf16[4,512,766]{2,1,0:T(8,128)(2,1)}) fusion(pred[512,766]{1,0:T(8,128)(4,1)S(1)} %fusion.16, bf16[512,4,64]{0,2,1:T(8,128)(2,1)S(1)} %bitcast.74, bf16[766,4,64]{0,2,1:T(8,128)(2,1)S(1)} %bitcast.72), kind=kOutput, calls=%fused_computation.86 | convolution fusion | flops 210215680 | bytes 4192256 | tf_op jit(solution)/shard_map/sub | solution.py:39
  205.7 3.1 %fusion.24 = bf16[512,4,64]{0,2,1:T(8,128)(2,1)S(1)} fusion(bf16[766,4,64]{0,2,1:T(8,128)(2,1)S(1)} %bitcast.68, bf16[4,512,766]{2,1,0:T(8,128)(2,1)} %get-tuple-element.16, f32[512,4]{0,1:T(4,128)S(1)} %divide_bitcast_fusion), kind=kOutput, calls=%fused_computation.29 | convolution fusion | flops 201064448 | bytes 3800064 | tf_op jit(solution)/shard_map/hqk,khd->qhd/dot_general | solution.py:41
  208.8 2.7 fusion.48
  211.5 39.9 %all-reduce.5.cloned.1.call-done = bf16[512,2048]{1,0:T(8,128)(2,1)} async-done(((bf16[512,2048]{1,0:T(8,128)(2,1)}), bf16[512,2048]{1,0:T(8,128)(2,1)}) %all-reduce.5.cloned.1.call-update) | async-done | bytes 2097168 | tf_op jit(solution)/shard_map/psum | solution.py:203
  251.4 12.2 %scatter_custom_fusion = f32[512,2048]{1,0:T(8,128)} fusion(f32[512,2048]{1,0:T(8,128)} %fusion.48, s32[512]{0:T(512)} %get-tuple-element.14, bf16[512,2048]{1,0:T(8,128)(2,1)} %all-reduce.5.cloned.1.call-done), kind=kCustom, calls=%fused_computation.7 | custom fusion | flops 2097152 | bytes 6291456 | tf_op jit(solution)/shard_map/scatter-add | solution.py:209
  263.6 3.8 %convert_element_type.55 = bf16[512,2048]{1,0:T(8,128)(2,1)} convert(f32[512,2048]{1,0:T(8,128)} %scatter_custom_fusion) | non-fusion elementwise | flops 1048576 | bytes 6291456 | tf_op jit(solution)/shard_map/convert_element_type | solution.py:211
  (73 shorter events, 28.5 us)
Async XLA Ops:
  6.5 191.7 %copy-start = (bf16[256,2048]{1,0:T(8,128)(2,1)S(1)}, bf16[256,2048]{1,0:T(8,128)(2,1)}, u32[]{:S(2)}) copy-start(bf16[256,2048]{1,0:T(8,128)(2,1)} %param.21) | copy-start | bytes 3145732
  6.5 63.4 %all-gather.2.cloned.1.call-start = ((), (), s32[]{:S(2)}) async-start(), calls=%async_computation.5 | async-start | bytes 10485760 | tf_op jit(solution)/shard_map/all_gather | solution.py:136
  12.2 66.6 %copy-start.8 = (pred[512]{0:T(512)(128)(4,1)}, pred[512]{0:T(512)(128)(4,1)S(1)}, u32[]{:S(2)}) copy-start(pred[512]{0:T(512)(128)(4,1)S(1)} %iota_compare_fusion.1) | copy-start | bytes 1540
  80.8 11.7 %copy-start.6 = (s32[1024]{0:T(1024)S(1)}, s32[1024]{0:T(1024)}, u32[]{:S(2)}) copy-start(s32[1024]{0:T(1024)} %param.13) | copy-start | bytes 12292
  83.6 20.2 %all-to-all-start = ((bf16[8,128,256]{2,1,0:T(8,128)(2,1)}), bf16[8,128,256]{2,1,0:T(8,128)(2,1)S(1)}, u32[]{:S(2)}, u32[]{:S(2)}) async-start(bf16[8,128,256]{2,1,0:T(8,128)(2,1)} %bitcast.11), calls=%async_computation | async-start | bytes 1048576 | tf_op jit(solution)/shard_map/all_to_all | solution.py:154
  93.1 6.5 %copy-start.3 = (bf16[2048,256]{1,0:T(8,128)(2,1)S(1)}, bf16[2048,256]{1,0:T(8,128)(2,1)}, u32[]{:S(2)}) copy-start(bf16[2048,256]{1,0:T(8,128)(2,1)} %param.19) | copy-start | bytes 3145732
  136.6 1.7 copy-start.1
  136.6 7.6 %copy-start.4 = (bf16[2048,256]{1,0:T(8,128)(2,1)S(1)}, bf16[2048,256]{1,0:T(8,128)(2,1)}, u32[]{:S(2)}) copy-start(bf16[2048,256]{1,0:T(8,128)(2,1)} %param.20) | copy-start | bytes 3145732
  140.4 10.3 %all-to-all-start.3 = ((f32[8,128,4]{1,2,0:T(4,128)}), f32[8,128,4]{1,2,0:T(4,128)S(1)}, u32[]{:S(2)}, u32[]{:S(2)}) async-start(f32[8,128,4]{1,2,0:T(4,128)} %bitcast.19), calls=%async_computation.3 | async-start | bytes 32768 | tf_op jit(solution)/shard_map/all_to_all | solution.py:169
  150.8 9.9 %all-to-all-start.2 = ((f32[8,128,4]{1,2,0:T(4,128)}), f32[8,128,4]{1,2,0:T(4,128)S(1)}, u32[]{:S(2)}, u32[]{:S(2)}) async-start(f32[8,128,4]{1,2,0:T(4,128)} %bitcast.16), calls=%async_computation.2 | async-start | bytes 32768 | tf_op jit(solution)/shard_map/all_to_all | solution.py:168
  160.7 21.9 %all-to-all-start.1 = ((f32[8,128,256]{1,2,0:T(8,128)}), f32[8,128,256]{1,2,0:T(8,128)S(1)}, u32[]{:S(2)}, u32[]{:S(2)}) async-start(f32[8,128,256]{1,2,0:T(8,128)} %copy.25), calls=%async_computation.1 | async-start | bytes 2097152 | tf_op jit(solution)/shard_map/all_to_all | solution.py:167
  164.2 2.8 %copy-start.2 = (bf16[512,2048]{1,0:T(8,128)(2,1)S(1)}, bf16[512,2048]{1,0:T(8,128)(2,1)}, u32[]{:S(2)}) copy-start(bf16[512,2048]{1,0:T(8,128)(2,1)} %param.11) | copy-start | bytes 6291460
  169.1 22.3 %collective-permute-start = (bf16[127,512]{0,1:T(8,128)(2,1)S(1)}, bf16[127,512]{0,1:T(8,128)(2,1)S(1)}, u32[]{:S(2)}, u32[]{:S(2)}) collective-permute-start(bf16[127,512]{0,1:T(8,128)(2,1)S(1)} %get-tuple-element.11), channel_id=1, source_target_pairs={{0,1},{1,2},{2,3},{3,4},{4,5},{5,6},{6,7},{7,8},{8,9},{9,10},{10,1... | collective-permute-start | bytes 390152 | tf_op jit(solution)/shard_map/ppermute | solution.py:19
  170.4 21.0 %collective-permute-start.1 = (bf16[127,512]{0,1:T(8,128)(2,1)S(1)}, bf16[127,512]{0,1:T(8,128)(2,1)S(1)}, u32[]{:S(2)}, u32[]{:S(2)}) collective-permute-start(bf16[127,512]{0,1:T(8,128)(2,1)S(1)} %get-tuple-element.12), channel_id=1, source_target_pairs={{1,0},{2,1},{3,2},{4,3},{5,4},{6,5},{7,6},{8,7},{9,8},{10,9},{11,1... | collective-permute-start | bytes 390152 | tf_op jit(solution)/shard_map/ppermute | solution.py:22
  183.7 14.5 %all-to-all-start.4 = ((bf16[8,128,256]{2,1,0:T(8,128)(2,1)}), bf16[8,128,256]{2,1,0:T(8,128)(2,1)S(1)}, u32[]{:S(2)}, u32[]{:S(2)}) async-start(bf16[8,128,256]{2,1,0:T(8,128)(2,1)} %broadcast_select_fusion), calls=%async_computation.4 | async-start | bytes 1048576 | tf_op jit(solution)/shard_map/all_to_all | solution.py:187
  187.3 64.0 %all-reduce.5.cloned.1.call-start = ((), (), s32[]{:S(2)}) async-start(), calls=%async_computation.6 | async-start | bytes 4194304 | tf_op jit(solution)/shard_map/psum | solution.py:203
  198.2 2.8 %copy-start.7 = (bf16[512,256]{0,1:T(8,128)(2,1)S(1)}, bf16[512,256]{0,1:T(8,128)(2,1)}, u32[]{:S(2)}) copy-start(bf16[512,256]{0,1:T(8,128)(2,1)} %convolution_convert_fusion) | copy-start | bytes 786436
  205.7 3.1 %copy-start.5 = (bf16[256,2048]{1,0:T(8,128)(2,1)S(1)}, bf16[256,2048]{1,0:T(8,128)(2,1)}, u32[]{:S(2)}) copy-start(bf16[256,2048]{1,0:T(8,128)(2,1)} %param.17) | copy-start | bytes 3145732
Sparse Core Ops, SparseCore 0:
  8.9 60.9 all-gather.1
  201.2 50.1 all-reduce.4
where the time goes:
time: 275 us; the launch traced here: 274 us
  waiting for transfers between devices  125 us (45%)
  blocking collectives  31.3 us (11%)
  matrix products  28 us (10%)
  other arithmetic  26.1 us (9%)
  local copies, waits for them, and re-layouts  24.2 us (9%)
  starting transfers between devices  22.3 us (8%)
  between operations  17.6 us (6%)
    all_gather x1, waiting for transfers between devices, shards(): block_rows = lax.all_gather(tokens, 'head', axis=0, tiled=True)  55.7 us
    psum x1, waiting for transfers between devices, shards(): lax.psum(head_term.astype(jnp.bfloat16), 'head').astype(jnp.float32)  39.9 us
    all_gather x1, blocking collectives, shards(): every_query = lax.all_gather(balanced, 'seq', axis=0, tiled=True)  31.3 us
    scatter-add x1, other arithmetic, shards(): jnp.zeros((row_count, model_width), jnp.float32).at[local_row]  12.2 us
    all_to_all x1, waiting for transfers between devices, shards(): lax.all_to_all(part_acc, 'seq', split_axis=0, concat_axis=0, tiled=True)  9.91 us
    gather x1, local copies, waits for them, and re-layouts, shards(): query_tokens = block_rows[query_place]  8.86 us
    gather x1, local copies, waits for them, and re-layouts, shards(): key_tokens = block_rows[key_place]  6.45 us
    all_to_all x1, waiting for transfers between devices, shards(): lax.all_to_all(outgoing.reshape(seq_count * share_len, heavy_width), 'seq...  6.3 us
  transfers between devices with their start and end apart: 9, of which 7 were waited for; matrix products, arithmetic and copies ran while one was open for 15% of the time, Pallas kernels for 0%

commit v1 on v0

v1 whole, which is shorter than its diff:
```python
import functools

import jax
import jax.numpy as jnp
from jax import lax
from jax.experimental import pallas as pl
from jax.experimental.pallas import tpu as pltpu
from jax.sharding import PartitionSpec as P

HDIM = 64
LHEADS = 4
RADIUS = 127
HALO = 128
FLOOR = -1e30
VMEM_LIMIT = 48 * 1024 * 1024


def softmax_mix(q, k, v, allowed):
    scores = lax.dot_general(
        q, k, (((1,), (1,)), ((), ())), preferred_element_type=jnp.float32
    ) * (HDIM**-0.5)
    scores = jnp.where(allowed, scores, FLOOR)
    peak = jnp.max(scores, axis=1, keepdims=True)
    weights = jnp.exp(scores - peak)
    total = jnp.sum(weights, axis=1, keepdims=True)
    mixed = jnp.dot(weights.astype(jnp.bfloat16), v, preferred_element_type=jnp.float32)
    return (mixed / total).astype(jnp.bfloat16)


def light_kernel(total_len, first_ref, q_ref, kv_ref, o_ref):
    rows, width = q_ref.shape
    span = 3 * HALO
    for tile in range(rows // HALO):
        start = tile * HALO
        q_off = lax.broadcasted_iota(jnp.int32, (HALO, span), 0) + HALO
        k_off = lax.broadcasted_iota(jnp.int32, (HALO, span), 1)
        key_pos = first_ref[0] + (start - HALO) + k_off
        allowed = (
            (jnp.abs(q_off - k_off) <= RADIUS) & (key_pos >= 0) & (key_pos < total_len)
        )
        for head in range(width // HDIM):
            cols = slice(head * HDIM, (head + 1) * HDIM)
            vcols = slice(width + head * HDIM, width + (head + 1) * HDIM)
            o_ref[start : start + HALO, cols] = softmax_mix(
                q_ref[start : start + HALO, cols],
                kv_ref[start : start + span, cols],
                kv_ref[start : start + span, vcols],
                allowed,
            )


def light_attention(first, queries, pairs, total_len):
    return pl.pallas_call(
        functools.partial(light_kernel, total_len),
        out_shape=jax.ShapeDtypeStruct(queries.shape, jnp.bfloat16),
        in_specs=[
            pl.BlockSpec(memory_space=pltpu.SMEM),
            pl.BlockSpec(memory_space=pltpu.VMEM),
            pl.BlockSpec(memory_space=pltpu.VMEM),
        ],
        out_specs=pl.BlockSpec(memory_space=pltpu.VMEM),
        compiler_params=pltpu.CompilerParams(vmem_limit_bytes=VMEM_LIMIT),
        cost_estimate=pl.CostEstimate(
            flops=8 * queries.shape[0] * 3 * HALO * queries.shape[1],
            bytes_accessed=4 * queries.size * 2,
            transcendentals=queries.shape[0] * 3 * HALO * LHEADS,
        ),
    )(first, queries, pairs)


def heavy_kernel(q_ref, kv_ref, valid_ref, o_ref):
    width = q_ref.shape[1]
    allowed = valid_ref[...] > 0
    for head in range(width // HDIM):
        cols = slice(head * HDIM, (head + 1) * HDIM)
        vcols = slice(width + head * HDIM, width + (head + 1) * HDIM)
        o_ref[:, cols] = softmax_mix(q_ref[:, cols], kv_ref[:, cols], kv_ref[:, vcols], allowed)


def heavy_attention(queries, pairs, valid):
    rows, width = queries.shape
    keys = pairs.shape[0]
    tile = 128
    return pl.pallas_call(
        heavy_kernel,
        grid=(rows // tile,),
        out_shape=jax.ShapeDtypeStruct(queries.shape, jnp.bfloat16),
        in_specs=[
            pl.BlockSpec((tile, width), lambda i: (i, 0)),
            pl.BlockSpec((keys, 2 * width), lambda i: (0, 0)),
            pl.BlockSpec((1, keys), lambda i: (0, 0)),
        ],
        out_specs=pl.BlockSpec((tile, width), lambda i: (i, 0)),
        compiler_params=pltpu.CompilerParams(vmem_limit_bytes=VMEM_LIMIT),
    )(queries, pairs, valid)


def dot16(a, b):
    return jnp.dot(a, b, preferred_element_type=jnp.float32).astype(jnp.bfloat16)


def block_runs(index, seq_count, block_len, cap, seq_rank):
    starts = jnp.arange(seq_count, dtype=jnp.int32) * block_len
    firsts = jnp.sum((index[None, :] < starts[:, None]).astype(jnp.int32), axis=1)
    ends = jnp.sum((index[None, :] < starts[:, None] + block_len).astype(jnp.int32), axis=1)
    counts = ends - firsts
    padded = jnp.concatenate([index, jnp.zeros((cap,), jnp.int32)])
    run = lax.dynamic_slice_in_dim(padded, firsts[seq_rank], cap, 0)
    valid = jnp.arange(cap, dtype=jnp.int32) < counts[seq_rank]
    place = jnp.where(valid, run - seq_rank * block_len, -1)
    return place, counts


def shards(
    tokens,
    query_index,
    key_index,
    light_query,
    light_key,
    light_value,
    light_out,
    heavy_query,
    heavy_key,
    heavy_value,
    heavy_out,
):
    row_count = tokens.shape[0]
    group_size = lax.axis_size("head")
    seq_count = lax.axis_size("seq")
    block_len = row_count * group_size
    seq_rank = lax.axis_index("seq")
    head_rank = lax.axis_index("head")
    my_first = (seq_rank * group_size + head_rank) * row_count
    total_len = block_len * seq_count
    query_cap = block_len // 4
    key_cap = 3 * block_len // 32
    light_width = light_query.shape[1]
    heavy_width = heavy_query.shape[1]

    block_rows = lax.all_gather(tokens, "head", axis=0, tiled=True)
    heavy_out_all = lax.all_gather(heavy_out, "head", axis=0, tiled=True)

    light_all = dot16(tokens, jnp.concatenate([light_query, light_key, light_value], axis=1))
    light_pair = light_all[:, light_width:]
    count = seq_count * group_size
    forward = [(i, i + 1) for i in range(count - 1)]
    backward = [(i + 1, i) for i in range(count - 1)]
    low = lax.ppermute(light_pair[row_count - HALO :], ("seq", "head"), forward)
    high = lax.ppermute(light_pair[:HALO], ("seq", "head"), backward)
    padded = jnp.concatenate([low, light_pair, high], axis=0)
    light_mixed = light_attention(
        my_first.reshape(1), light_all[:, :light_width], padded, total_len
    )

    query_place, _ = block_runs(query_index, seq_count, block_len, query_cap, seq_rank)
    key_place, key_counts = block_runs(key_index, seq_count, block_len, key_cap, seq_rank)
    block_ids = jnp.arange(block_len, dtype=jnp.int32)
    query_pick = (query_place[:, None] == block_ids[None, :]).astype(jnp.bfloat16)
    key_pick = (key_place[:, None] == block_ids[None, :]).astype(jnp.bfloat16)
    local_ids = head_rank * row_count + jnp.arange(row_count, dtype=jnp.int32)
    place_back = (local_ids[:, None] == query_place[None, :]).astype(jnp.bfloat16)
    valid = (jnp.arange(key_cap, dtype=jnp.int32)[None, :] < key_counts[:, None]).astype(
        jnp.int32
    ).reshape(1, seq_count * key_cap)

    projected = dot16(block_rows, jnp.concatenate([heavy_key, heavy_value, heavy_query], axis=1))
    routed_pair = dot16(key_pick, projected[:, : 2 * heavy_width])
    every_pair = lax.all_gather(routed_pair, "seq", axis=0, tiled=True)
    routed_q = dot16(query_pick, projected[:, 2 * heavy_width :])
    mixed = heavy_attention(routed_q, every_pair, valid)
    every_mixed = lax.all_gather(mixed, "head", axis=1, tiled=True)
    heavy_mixed = dot16(place_back, every_mixed)
    return dot16(
        jnp.concatenate([light_mixed, heavy_mixed], axis=1),
        jnp.concatenate([light_out, heavy_out_all], axis=0),
    )


def solution(mesh):
    placed = (
        P(("seq", "head"), None),
        P(),
        P(),
        P(),
        P(),
        P(),
        P(),
        P(None, "head"),
        P(None, "head"),
        P(None, "head"),
        P("head", None),
    )
    return jax.shard_map(
        shards, mesh=mesh, in_specs=placed, out_specs=P(("seq", "head"), None), check_vma=False
    )
```

time: 275 us -> 206 us (0.75)
  blocking collectives: 31.3 us -> 0 us
  other arithmetic: 26.1 us -> 3.17 us
  starting transfers between devices: 22.3 us -> 2.89 us
  local copies, waits for them, and re-layouts: 24.2 us -> 5.61 us
  Pallas kernels: 0 us -> 13.7 us
  waiting for transfers between devices: 125 us -> 137 us
    all_gather x0 -> x3, waiting for transfers between devices: none -> 75.5 us  [the longest x1 38.2 us: shards(): every_pair = lax.all_gather(routed_pair, 'seq', axis=0, tiled=True)]
    psum x1 -> x0, waiting for transfers between devices: 39.9 us -> none  [shards(): lax.psum(head_term.astype(jnp.bfloat16), 'head').astype(jnp.float32)]
    all_gather x1 -> x0, blocking collectives: 31.3 us -> none  [shards(): every_query = lax.all_gather(balanced, 'seq', axis=0, tiled=True)]
    all_to_all x5 -> x0, waiting for transfers between devices: 28.5 us -> none  [the longest x1 9.91 us: shards(): lax.all_to_all(part_acc, 'seq', split_axis=0, concat_axis=0, tiled=True)]
    all_to_all x5 -> x0, starting transfers between devices: 19.5 us -> none  [the longest x1 5.28 us: shards(): lax.all_to_all(dense, 'seq', split_axis=0, concat_axis=0, tiled=True)]
    gather x2 -> x0, local copies, waits for them, and re-layouts: 15.3 us -> none  [the longest x1 8.86 us: shards(): query_tokens = block_rows[query_place]]
    pallas_call x0 -> x2, Pallas kernels: none -> 13.7 us  [the longest x1 8.78 us: heavy_attention(): pl.pallas_call(heavy_kernel, grid=(rows // tile,), out_shape=jax.ShapeDty...]
    scatter-add x1 -> x0, other arithmetic: 12.2 us -> none  [shards(): jnp.zeros((row_count, model_width), jnp.float32).at[local_row]]
  transfers between devices with their start and end apart: 9 -> 6, of which waited for: 7 -> 5; matrix products, arithmetic and copies ran while one was open for 15% -> 6% of each run, Pallas kernels for 0% -> 2%
where the time goes in v1:
time: 206 us; the launch traced here: 205 us
  waiting for transfers between devices  137 us (67%)
  matrix products  25.6 us (12%)
  between operations  16.9 us (8%)
  Pallas kernels  13.7 us (7%)
  local copies, waits for them, and re-layouts  5.61 us (3%)
  other arithmetic  3.17 us (2%)
  starting transfers between devices  2.89 us (1%)
    all_gather x1, waiting for transfers between devices, shards(): block_rows = lax.all_gather(tokens, 'head', axis=0, tiled=True)  57.2 us
    all_gather x1, waiting for transfers between devices, shards(): every_pair = lax.all_gather(routed_pair, 'seq', axis=0, tiled=True)  38.2 us
    all_gather x1, waiting for transfers between devices, shards(): heavy_out_all = lax.all_gather(heavy_out, 'head', axis=0, tiled=True)  33.9 us
    dot_general x6, matrix products, dot16(): jnp.dot(a, b, preferred_element_type=jnp.float32).astype(jnp.bfloat16)  25.6 us
    pallas_call x1, Pallas kernels, heavy_attention(): pl.pallas_call(heavy_kernel, grid=(rows // tile,), out_shape=jax.ShapeDty...  8.78 us
    pallas_call x1, Pallas kernels, light_attention(): pl.pallas_call(functools.partial(light_kernel, total_len), out_shape=jax....  4.96 us
  transfers between devices with their start and end apart: 6, of which 5 were waited for; matrix products, arithmetic and copies ran while one was open for 6% of the time, Pallas kernels for 2%

profile of v1, /device:TPU:0, one launch (start us, length us, event | category | flops | bytes accessed | tf_op | source)
XLA Modules:
  0.0 205.2 jit_solution(8030687018605776925)
XLA Ops:
  6.5 0.7 all-gather.5.cloned.1.call-update
  7.3 0.9 convert_reduce_fusion.3
  8.2 0.6 dynamic_slice.22
  10.2 0.6 dynamic_slice.21
  11.4 1.3 compare_select_fusion
  12.7 57.2 %all-gather.5.cloned.1.call-done = bf16[2048,2048]{1,0:T(8,128)(2,1)} async-done(((bf16[512,2048]{1,0:T(8,128)(2,1)}), bf16[2048,2048]{1,0:T(8,128)(2,1)}) %all-gather.5.cloned.1.call-update) | async-done | bytes 8388624 | tf_op jit(solution)/shard_map/all_gather | solution.py:140
  69.9 10.1 %fusion.16 = bf16[2048,768]{0,1:T(8,128)(2,1)S(1)} fusion(bf16[2048,2048]{1,0:T(8,128)(2,1)} %all-gather.5.cloned.1.call-done, bf16[2048,256]{1,0:T(8,128)(2,1)} %param.18, bf16[2048,256]{1,0:T(8,128)(2,1)} %param.20, bf16[2048,256]{1,0:T(8,128)(2,1)} %param.19), kind=kOutput, calls=%fused_computation.18 | convolution fusion | flops 6453460992 | bytes 14680064 | tf_op jit(solution)/shard_map/dot_general | solution.py:99
  80.0 1.6 copy-done.5
  81.6 1.5 fusion.35
  84.9 0.7 dynamic_slice.18
  86.3 0.8 fusion.45
  87.1 2.2 %fusion.34.q_ref = bf16[512,256]{1,0:T(8,128)(2,1)S(1)} fusion(s32[512]{0:T(512)S(1)} %fusion.45, bf16[2048,768]{0,1:T(8,128)(2,1)} %copy-done.5), kind=kOutput, calls=%fused_computation.30 | convolution fusion | flops 538050560 | bytes 1312768 | tf_op jit(solution)/shard_map/dot_general | solution.py:99
  89.3 38.2 %all-gather.7.cloned.1.call-done.kv_ref = bf16[1536,512]{1,0:T(8,128)(2,1)} async-done(((bf16[192,512]{1,0:T(8,128)(2,1)}), bf16[1536,512]{1,0:T(8,128)(2,1)}) %all-gather.7.cloned.1.call-update) | async-done | bytes 1572880 | tf_op jit(solution)/shard_map/all_gather | solution.py:168
  127.5 1.4 copy-done
  128.9 8.8 %shard_map.110 = bf16[512,256]{1,0:T(8,128)(2,1)} custom-call(bf16[512,256]{1,0:T(8,128)(2,1)S(1)} %fusion.34.q_ref, bf16[1536,512]{1,0:T(8,128)(2,1)S(1)} %copy-done, s32[1,1536]{1,0:T(1,128)S(1)} %reshape.54.valid_ref), custom_call_target="tpu_custom_call" | custom-call | tf_op jit(solution)/shard_map/pallas_call | solution.py:84
  138.4 3.3 %fusion.31 = bf16[512,768]{1,0:T(8,128)(2,1)S(1)} fusion(bf16[512,2048]{1,0:T(8,128)(2,1)S(1)} %copy-done.1, bf16[2048,256]{1,0:T(8,128)(2,1)S(1)} %copy-done.3, bf16[2048,256]{1,0:T(8,128)(2,1)} %param.15, bf16[2048,256]{1,0:T(8,128)(2,1)} %param.14), kind=kOutput, calls=%fused_computation.29 | convolution fusion | flops 1620443136 | bytes 6029312 | tf_op jit(solution)/shard_map/dot_general | solution.py:99
  141.7 1.3 collective-permute-start
  143.0 1.5 collective-permute-start.1
  144.6 3.3 %collective-permute-done.1 = bf16[128,512]{1,0:T(8,128)(2,1)S(1)} collective-permute-done((bf16[128,512]{1,0:T(8,128)(2,1)S(1)}, bf16[128,512]{1,0:T(8,128)(2,1)S(1)}, u32[]{:S(2)}, u32[]{:S(2)}) %collective-permute-start.1) | collective-permute-done | bytes 131104 | tf_op jit(solution)/shard_map/ppermute | solution.py:149
  148.0 5.0 %shard_map.109 = bf16[512,256]{1,0:T(8,128)(2,1)S(1)} custom-call(s32[1]{0:T(128)} %bitcast.first_ref, bf16[512,256]{1,0:T(8,128)(2,1)S(1)} %slice.26.q_ref, bf16[768,512]{1,0:T(8,128)(2,1)S(1)} %pad_maximum_fusion.kv_ref), custom_call_target="tpu_custom_call" | custom-call | flops 402653184 | bytes 1048576 | tf_op jit(solution)/shard_map/pallas_call | solution.py:53
  153.0 3.4 %all-gather.9.cloned.1.call-done = bf16[512,1024]{1,0:T(8,128)(2,1)} async-done(((bf16[512,256]{1,0:T(8,128)(2,1)}), bf16[512,1024]{1,0:T(8,128)(2,1)}) %all-gather.9.cloned.1.call-update) | async-done | bytes 1048592 | tf_op jit(solution)/shard_map/all_gather | solution.py:171
  156.4 2.0 convolution_convert_fusion.1
  158.3 33.9 %all-gather.11.cloned.1.call-done = bf16[1024,2048]{1,0:T(8,128)(2,1)} async-done(((bf16[256,2048]{1,0:T(8,128)(2,1)}), bf16[1024,2048]{1,0:T(8,128)(2,1)}) %all-gather.11.cloned.1.call-update) | async-done | bytes 4194320 | tf_op jit(solution)/shard_map/all_gather | solution.py:141
  192.3 6.4 %fusion.19 = bf16[512,2048]{1,0:T(8,128)(2,1)} fusion(bf16[1024,2048]{1,0:T(8,128)(2,1)} %all-gather.11.cloned.1.call-done, bf16[256,2048]{1,0:T(8,128)(2,1)S(1)} %copy-done.4, bf16[512,1024]{1,0:T(8,128)(2,1)S(1)} %convolution_convert_fusion.1, bf16[512,256]{1,0:T(8,128)(2,1)S(1)} %shard_map.109), kind=kOutput, calls=%fused_computation.19 | convolution fusion | flops 2698510336 | bytes 8650752 | tf_op jit(solution)/shard_map/dot_general | solution.py:99
  (29 shorter events, 1.6 us)
Async XLA Ops:
  6.5 63.4 %all-gather.5.cloned.1.call-start = ((), (), s32[]{:S(2)}) async-start(), calls=%async_computation | async-start | bytes 10485760 | tf_op jit(solution)/shard_map/all_gather | solution.py:140
  7.3 120.3 %all-gather.7.cloned.1.call-start = ((), (), s32[]{:S(2)}) async-start(), calls=%async_computation.1 | async-start | bytes 1769472 | tf_op jit(solution)/shard_map/all_gather | solution.py:168
  80.0 1.6 copy-start.5
  81.6 4.6 %copy-start.2 = (s32[1024]{0:T(1024)S(1)}, s32[1024]{0:T(1024)}, u32[]{:S(2)}) copy-start(s32[1024]{0:T(1024)} %param.12) | copy-start | bytes 12292
  83.2 73.2 %all-gather.9.cloned.1.call-start = ((), (), s32[]{:S(2)}) async-start(), calls=%async_computation.2 | async-start | bytes 1310720 | tf_op jit(solution)/shard_map/all_gather | solution.py:171
  87.1 51.3 %copy-start.1 = (bf16[512,2048]{1,0:T(8,128)(2,1)S(1)}, bf16[512,2048]{1,0:T(8,128)(2,1)}, u32[]{:S(2)}) copy-start(bf16[512,2048]{1,0:T(8,128)(2,1)} %param.11) | copy-start | bytes 6291460
  87.1 51.3 %copy-start.3 = (bf16[2048,256]{1,0:T(8,128)(2,1)S(1)}, bf16[2048,256]{1,0:T(8,128)(2,1)}, u32[]{:S(2)}) copy-start(bf16[2048,256]{1,0:T(8,128)(2,1)} %param.16) | copy-start | bytes 3145732
  127.5 1.4 copy-start
  137.8 54.5 %all-gather.11.cloned.1.call-start = ((), (), s32[]{:S(2)}) async-start(), calls=%async_computation.3 | async-start | bytes 5242880 | tf_op jit(solution)/shard_map/all_gather | solution.py:141
  141.7 2.9 %collective-permute-start = (bf16[128,512]{1,0:T(8,128)(2,1)S(1)}, bf16[128,512]{1,0:T(8,128)(2,1)S(1)}, u32[]{:S(2)}, u32[]{:S(2)}) collective-permute-start(bf16[128,512]{1,0:T(8,128)(2,1)S(1)} %get-tuple-element.11), channel_id=1, source_target_pairs={{0,1},{1,2},{2,3},{3,4},{4,5},{5,6},{6,7},{7,8},{8,9},{9,10},{10,1... | collective-permute-start | bytes 393224 | tf_op jit(solution)/shard_map/ppermute | solution.py:148
  143.0 4.9 %collective-permute-start.1 = (bf16[128,512]{1,0:T(8,128)(2,1)S(1)}, bf16[128,512]{1,0:T(8,128)(2,1)S(1)}, u32[]{:S(2)}, u32[]{:S(2)}) collective-permute-start(bf16[128,512]{1,0:T(8,128)(2,1)S(1)} %get-tuple-element.12), channel_id=1, source_target_pairs={{1,0},{2,1},{3,2},{4,3},{5,4},{6,5},{7,6},{8,7},{9,8},{10,9},{11,1... | collective-permute-start | bytes 393224 | tf_op jit(solution)/shard_map/ppermute | solution.py:149
  144.6 47.7 %copy-start.4 = (bf16[256,2048]{1,0:T(8,128)(2,1)S(1)}, bf16[256,2048]{1,0:T(8,128)(2,1)}, u32[]{:S(2)}) copy-start(bf16[256,2048]{1,0:T(8,128)(2,1)} %param.17) | copy-start | bytes 3145732
Sparse Core Ops, SparseCore 0:
  8.9 60.9 all-gather.4
  83.3 44.1 all-gather.6
  137.9 18.4 all-gather.8
  157.8 34.4 all-gather.10

commit v2 on v1

v2 whole, which is shorter than its diff:
```python
import functools

import jax
import jax.numpy as jnp
from jax import lax
from jax.experimental import pallas as pl
from jax.experimental.pallas import tpu as pltpu
from jax.sharding import PartitionSpec as P

HDIM = 64
RADIUS = 127
HALO = 128
TILE = 128
FLOOR = -1e30
VMEM_LIMIT = 60 * 1024 * 1024
MESH = pl.DeviceIdType.MESH


def dot32(a, b):
    return jnp.dot(a, b, preferred_element_type=jnp.float32)


def dot16(a, b):
    return dot32(a, b).astype(jnp.bfloat16)


def softmax_mix(q, k, v, allowed):
    scores = lax.dot_general(
        q, k, (((1,), (1,)), ((), ())), preferred_element_type=jnp.float32
    ) * (HDIM**-0.5)
    scores = jnp.where(allowed, scores, FLOOR)
    peak = jnp.max(scores, axis=1, keepdims=True)
    weights = jnp.exp(scores - peak)
    total = jnp.sum(weights, axis=1, keepdims=True)
    mixed = dot32(weights.astype(jnp.bfloat16), v)
    return (mixed / total).astype(jnp.bfloat16)


def slot_places(index_ref, cap, first_token):
    total = index_ref.shape[1]
    piece = min(total, 1024)
    before = jnp.zeros((1, 1), jnp.int32)
    for start in range(0, total, piece):
        part = index_ref[:, start : start + piece]
        before += jnp.sum((part < first_token).astype(jnp.int32), axis=1, keepdims=True)
    place = jnp.zeros((cap, 1), jnp.int32)
    for start in range(0, total, piece):
        part = index_ref[:, start : start + piece]
        rank = lax.broadcasted_iota(jnp.int32, (cap, piece), 1) + (start - before)
        slot = lax.broadcasted_iota(jnp.int32, (cap, piece), 0)
        place += jnp.sum(jnp.where(rank == slot, part + 1, 0), axis=1, keepdims=True)
    return place - 1 - first_token


def key_mask(index_ref, seq_count, cap, block_len):
    position = lax.broadcasted_iota(jnp.int32, (1, seq_count * cap), 1)
    index = index_ref[...]
    mask = jnp.zeros((1, seq_count * cap), jnp.int32)
    for block in range(seq_count):
        inside = (index >= block * block_len) & (index < (block + 1) * block_len)
        count = jnp.sum(inside.astype(jnp.int32), axis=1, keepdims=True)
        hit = (position >= block * cap) & (position < block * cap + count)
        mask = mask | hit.astype(jnp.int32)
    return mask


def kernel(
    seq_count,
    group,
    tok,
    qi,
    ki,
    lq,
    lk,
    lv,
    lo,
    hq,
    hk,
    hv,
    ho,
    out,
    got_tok,
    place_ref,
    mask_ref,
    pick,
    pick_x,
    pick_core,
    light_q,
    light_kv,
    light_mix,
    pairs,
    queries,
    mix,
    walls,
    placed,
    send,
    recv,
):
    rows, width = tok.shape
    half = width // 2
    block_len = rows * group
    total_len = block_len * seq_count
    query_cap = queries.shape[0]
    key_cap = pairs.shape[1]
    hw = hq.shape[1]
    lw = lq.shape[1]
    zs = seq_count // 2
    s, h = lax.axis_index("seq"), lax.axis_index("head")
    x, c = h // 2, h % 2
    z, y = s // 2, s % 2
    core = (s, x * 2 + 1 - c)
    xp = (s, (1 - x) * 2 + c)
    yp = (z * 2 + 1 - y, h)
    zp = [None] + [(((z + d) % zs) * 2 + y, h) for d in range(1, zs)]
    flat, count = s * group + h, seq_count * group
    up, down = (flat + 1) % count, (flat + count - 1) % count
    above, below = (up // group, up % group), (down // group, down % group)
    partners = [core, xp, yp, above, below] + zp[1:]

    barrier = pltpu.get_barrier_semaphore()
    for device in partners:
        pl.semaphore_signal(barrier, inc=1, device_id=device, device_id_type=MESH)
    pl.semaphore_wait(barrier, len(partners))

    used = [0]
    begun = []

    def remote(src, dst, device):
        number = used[0]
        used[0] += 1
        copy = pltpu.make_async_remote_copy(
            src_ref=src,
            dst_ref=dst,
            send_sem=send.at[number],
            recv_sem=recv.at[number],
            device_id=device,
            device_id_type=MESH,
        )
        begun.append(copy)
        return copy

    mine = pl.multiple_of(c * half, half)
    other = pl.multiple_of((1 - c) * half, half)
    tok_copy = remote(tok.at[:, pl.ds(other, half)], got_tok, core)
    tok_copy.start()

    first_token = s * block_len
    place_ref[:key_cap] = slot_places(ki, key_cap, first_token)
    place_ref[key_cap:] = slot_places(qi, query_cap, first_token)
    mask_ref[...] = key_mask(ki, seq_count, key_cap, block_len)

    def chosen(start, size, owner):
        ids = lax.broadcasted_iota(jnp.int32, (size, rows), 1) + owner * rows
        hit = place_ref[start : start + size] == ids
        return hit.astype(jnp.float32).astype(jnp.bfloat16)

    def choose(start, size):
        pick[start : start + size] = (
            dot32(chosen(start, size, h), tok[:, pl.ds(mine, half)])
            + dot32(chosen(start, size, core[1]), got_tok[...])
        ).astype(jnp.bfloat16)

    tok_copy.wait_recv()
    choose(0, key_cap)
    span = pl.ds(0, key_cap)
    key_x = remote(pick.at[span], pick_x.at[span], xp)
    key_x.start()
    wall_core = remote(ho, walls.at[0], core)
    wall_core.start()

    spans = [(key_cap + i * TILE, TILE) for i in range(query_cap // TILE)]
    for start, size in spans:
        choose(start, size)

    def light_project(tile, carry):
        at = pl.multiple_of(tile * TILE, TILE)
        part = tok[pl.ds(at, TILE)]
        light_q[pl.ds(at, TILE)] = dot16(part, lq[...])
        light_kv[pl.ds(at + HALO, TILE), :lw] = dot16(part, lk[...])
        light_kv[pl.ds(at + HALO, TILE), lw:] = dot16(part, lv[...])
        return carry

    lax.fori_loop(0, rows // TILE, light_project, 0)
    to_above = remote(light_kv.at[pl.ds(rows, HALO)], light_kv.at[pl.ds(0, HALO)], above)
    to_above.start()
    to_below = remote(
        light_kv.at[pl.ds(HALO, HALO)], light_kv.at[pl.ds(rows + HALO, HALO)], below
    )
    to_below.start()

    key_x.wait()
    part_rows = ho.shape[0] // 2
    wall_part = pl.ds(pl.multiple_of(y * part_rows, part_rows), part_rows)
    wall_rest = pl.ds(pl.multiple_of((1 - y) * part_rows, part_rows), part_rows)
    wall_x = remote(ho.at[wall_part], walls.at[1, wall_part], xp)
    wall_x.start()

    def join(start, size):
        rows_here = pl.ds(start, size)
        pick[rows_here] = pick[rows_here] + pick_x[rows_here]
        copy = remote(pick.at[rows_here], pick_core.at[rows_here], core)
        copy.start()
        return copy

    def project(start, size, matrix):
        return (
            dot32(pick[start : start + size], matrix[pl.ds(mine, half)])
            + dot32(pick_core[start : start + size], matrix[pl.ds(other, half)])
        ).astype(jnp.bfloat16)

    key_core = join(0, key_cap)
    query_x = []
    for start, size in spans:
        copy = remote(pick.at[pl.ds(start, size)], pick_x.at[pl.ds(start, size)], xp)
        copy.start()
        query_x.append(copy)
    key_core.wait_recv()
    pairs[s, :, :hw] = project(0, key_cap, hk)
    pairs[s, :, hw:] = project(0, key_cap, hv)
    pair_z = [None]
    for d in range(1, zs):
        copy = remote(pairs.at[s], pairs.at[s], zp[d])
        copy.start()
        pair_z.append(copy)
    pair_y = [remote(pairs.at[s], pairs.at[s], yp)]
    pair_y[0].start()

    to_above.wait_recv()
    to_below.wait_recv()
    reach = 3 * HALO
    q_off = lax.broadcasted_iota(jnp.int32, (HALO, reach), 0) + HALO
    k_off = lax.broadcasted_iota(jnp.int32, (HALO, reach), 1)
    near = jnp.abs(q_off - k_off) <= RADIUS

    def light_tile(tile, carry):
        at = pl.multiple_of(tile * HALO, HALO)
        key_pos = flat * rows + (at - HALO) + k_off
        allowed = near & (key_pos >= 0) & (key_pos < total_len)
        for head in range(lw // HDIM):
            lo_col, hi_col = head * HDIM, (head + 1) * HDIM
            light_mix[pl.ds(at, HALO), lo_col:hi_col] = softmax_mix(
                light_q[pl.ds(at, HALO), lo_col:hi_col],
                light_kv[pl.ds(at, reach), lo_col:hi_col],
                light_kv[pl.ds(at, reach), lw + lo_col : lw + hi_col],
                allowed,
            )
        return carry

    lax.fori_loop(0, rows // HALO, light_tile, 0)

    for d in range(1, zs):
        pair_z[d].wait_recv()
        slot = ((z + zs - d) % zs) * 2 + y
        copy = remote(pairs.at[slot], pairs.at[slot], yp)
        copy.start()
        pair_y.append(copy)

    wall_x.wait_recv()
    wall_y = remote(walls.at[1, wall_part], walls.at[1, wall_part], yp)
    wall_y.start()
    wall_core_a = remote(walls.at[1, wall_part], walls.at[2, wall_part], core)
    wall_core_a.start()

    query_core = []
    for i, (start, size) in enumerate(spans):
        query_x[i].wait()
        query_core.append(join(start, size))
    for copy in pair_y:
        copy.wait_recv()

    keys = seq_count * key_cap
    step = TILE if keys <= 2048 else 32
    mix_x, mix_core, mix_far = [], [], []
    for i, (start, size) in enumerate(spans):
        at = start - key_cap
        query_core[i].wait_recv()
        queries[at : at + size] = project(start, size, hq)

        def heavy_tile(tile, carry):
            here = pl.multiple_of(at + tile * step, step)
            for head in range(hw // HDIM):
                lo_col, hi_col = head * HDIM, (head + 1) * HDIM
                mix[0, pl.ds(here, step), lo_col:hi_col] = softmax_mix(
                    queries[pl.ds(here, step), lo_col:hi_col],
                    pairs[:, :, lo_col:hi_col].reshape(keys, HDIM),
                    pairs[:, :, hw + lo_col : hw + hi_col].reshape(keys, HDIM),
                    mask_ref[...] > 0,
                )
            return carry

        lax.fori_loop(0, size // step, heavy_tile, 0)
        here = pl.ds(at, size)
        mix_x.append(remote(mix.at[0, here], mix.at[2, here], xp))
        mix_x[-1].start()
        mix_core.append(remote(mix.at[0, here], mix.at[1, here], core))
        mix_core[-1].start()
        if i == 0:
            wall_y.wait_recv()
            wall_core_b = remote(walls.at[1, wall_rest], walls.at[2, wall_rest], core)
            wall_core_b.start()
        else:
            mix_x[i - 1].wait_recv()
            before = pl.ds(at - TILE, TILE)
            mix_far.append(remote(mix.at[2, before], mix.at[3, before], core))
            mix_far[-1].start()
    mix_x[-1].wait_recv()
    last = pl.ds(query_cap - TILE, TILE)
    mix_far.append(remote(mix.at[2, last], mix.at[3, last], core))
    mix_far[-1].start()

    def back(part):
        pick_t = chosen(key_cap, query_cap, h)
        placed[part] = lax.dot_general(
            pick_t, mix[part], (((0,), (0,)), ((), ())), preferred_element_type=jnp.float32
        ).astype(jnp.bfloat16)

    back(0)
    for copy in mix_core:
        copy.wait_recv()
    back(1)
    back(2)
    for copy in mix_far:
        copy.wait_recv()
    back(3)
    wall_core.wait_recv()
    wall_core_a.wait_recv()
    wall_core_b.wait_recv()

    def finish(tile, carry):
        here = pl.ds(pl.multiple_of(tile * TILE, TILE), TILE)
        out[here] = (
            dot32(light_mix[here], lo[...])
            + dot32(placed[0, here], ho[...])
            + dot32(placed[1, here], walls[0])
            + dot32(placed[2, here], walls[1])
            + dot32(placed[3, here], walls[2])
        ).astype(jnp.bfloat16)
        return carry

    lax.fori_loop(0, rows // TILE, finish, 0)

    waited = [key_x] + query_x
    for copy in begun:
        if not any(copy is done for done in waited):
            copy.wait_send()


def shards(tokens, query_index, key_index, *weights):
    seq_count, group = lax.axis_size("seq"), lax.axis_size("head")
    rows, width = tokens.shape
    lw, hw = weights[0].shape[1], weights[4].shape[1]
    block_len = rows * group
    query_cap, key_cap = block_len // 4, 3 * block_len // 32
    slots = query_cap + key_cap
    copies = 8 + 2 * (seq_count // 2) + 5 * (query_cap // TILE) + 8
    bf16 = jnp.bfloat16
    return pl.pallas_call(
        functools.partial(kernel, seq_count, group),
        out_shape=jax.ShapeDtypeStruct(tokens.shape, bf16),
        in_specs=[pl.BlockSpec(memory_space=pltpu.VMEM)] * 11,
        out_specs=pl.BlockSpec(memory_space=pltpu.VMEM),
        scratch_shapes=[
            pltpu.VMEM((rows, width // 2), bf16),
            pltpu.VMEM((slots, 1), jnp.int32),
            pltpu.VMEM((1, seq_count * key_cap), jnp.int32),
            pltpu.VMEM((slots, width // 2), bf16),
            pltpu.VMEM((slots, width // 2), bf16),
            pltpu.VMEM((slots, width // 2), bf16),
            pltpu.VMEM((rows, lw), bf16),
            pltpu.VMEM((rows + 2 * HALO, 2 * lw), bf16),
            pltpu.VMEM((rows, lw), bf16),
            pltpu.VMEM((seq_count, key_cap, 2 * hw), bf16),
            pltpu.VMEM((query_cap, hw), bf16),
            pltpu.VMEM((4, query_cap, hw), bf16),
            pltpu.VMEM((3,) + weights[7].shape, bf16),
            pltpu.VMEM((4, rows, hw), bf16),
            pltpu.SemaphoreType.DMA((copies,)),
            pltpu.SemaphoreType.DMA((copies,)),
        ],
        compiler_params=pltpu.CompilerParams(
            collective_id=0, has_side_effects=True, vmem_limit_bytes=VMEM_LIMIT
        ),
    )(tokens, query_index.reshape(1, -1), key_index.reshape(1, -1), *weights)


def solution(mesh):
    placed = (
        P(("seq", "head"), None),
        P(),
        P(),
        P(),
        P(),
        P(),
        P(),
        P(None, "head"),
        P(None, "head"),
        P(None, "head"),
        P("head", None),
    )
    return jax.shard_map(
        shards, mesh=mesh, in_specs=placed, out_specs=P(("seq", "head"), None), check_vma=False
    )
```

time: 206 us -> 86.1 us (0.42)
  waiting for transfers between devices: 137 us -> 0 us
  Pallas kernels: 13.7 us -> 82.2 us
  matrix products: 25.6 us -> 0 us
  between operations: 16.9 us -> 0.01 us
  other arithmetic: 3.17 us -> 0 us
  starting transfers between devices: 2.89 us -> 0 us
  local copies, waits for them, and re-layouts: 5.61 us -> 3.16 us
    all_gather x4 -> x0, waiting for transfers between devices: 133 us -> none  [the longest x1 57.2 us: shards(): block_rows = lax.all_gather(tokens, 'head', axis=0, tiled=True)]
    pallas_call x2 -> x1, Pallas kernels: 13.7 us -> 82.2 us  [shards(): pl.pallas_call(functools.partial(kernel, seq_count, group), out_shape=jax...]
    dot_general x6 -> x0, matrix products: 25.6 us -> none  [dot16(): jnp.dot(a, b, preferred_element_type=jnp.float32).astype(jnp.bfloat16)]
    ppermute x2 -> x0, waiting for transfers between devices: 3.33 us -> none  [the longest x1 3.33 us: shards(): high = lax.ppermute(light_pair[:HALO], ('seq', 'head'), backward)]
    ppermute x2 -> x0, starting transfers between devices: 2.77 us -> none  [the longest x1 1.47 us: shards(): high = lax.ppermute(light_pair[:HALO], ('seq', 'head'), backward)]
    dynamic_slice x4 -> x0, local copies, waits for them, and re-layouts: 2.41 us -> none  [the longest x2 1.26 us: block_runs(): valid = jnp.arange(cap, dtype=jnp.int32) < counts[seq_rank]]
    select_n x2 -> x0, other arithmetic: 2.1 us -> none  [block_runs(): place = jnp.where(valid, run - seq_rank * block_len, -1)]
  transfers between devices with their start and end apart: 6 -> 0, of which waited for: 5 -> 0; matrix products, arithmetic and copies ran while one was open for 6% -> 0% of each run, Pallas kernels for 2% -> 0%
where the time goes in v2:
time: 86.1 us; the launch traced here: 85.4 us
  Pallas kernels  82.2 us (95%)
  local copies, waits for them, and re-layouts  3.16 us (4%)
    pallas_call x1, Pallas kernels, shards(): pl.pallas_call(functools.partial(kernel, seq_count, group), out_shape=jax...  82.2 us
    unnamed x1, local copies, waits for them, and re-layouts  3.16 us

profile of v2, /device:TPU:0, one launch (start us, length us, event | category | flops | bytes accessed | tf_op | source)
XLA Modules:
  0.0 85.4 jit_solution(14013471194590263638)
XLA Ops:
  0.0 82.2 %shard_map.109 = bf16[512,2048]{1,0:T(8,128)(2,1)} custom-call(bf16[512,2048]{1,0:T(8,128)(2,1)} %tok.1, s32[1,1024]{1,0:T(1,128)} %bitcast.2, s32[1,1024]{1,0:T(1,128)} %bitcast.3, bf16[2048,256]{1,0:T(8,128)(2,1)} %lq.1, bf16[2048,256]{1,0:T(8,128)(2,1)} %lk.1, bf16[2048,256]{1,0:T(8,128)(2,1)} %lv.1, bf16[256,2048]{1,0:T(8,128)(2,1)} %lo.1, ...), custom_call_target="tpu_custom_call" | custom-call | tf_op jit(solution)/shard_map/pallas_call | solution.py:357
  82.2 3.2 %copy.13 = bf16[512,2048]{1,0:T(8,128)(2,1)} copy(bf16[512,2048]{1,0:T(8,128)(2,1)} %shard_map.109) | data formatting | bytes 4194304

commit v3 on v2

--- a/solution.py
+++ b/solution.py
@@ -24,11 +24,10 @@
     return dot32(a, b).astype(jnp.bfloat16)
 
 
-def softmax_mix(q, k, v, allowed):
+def softmax_mix(q, k, v, bias):
     scores = lax.dot_general(
         q, k, (((1,), (1,)), ((), ())), preferred_element_type=jnp.float32
-    ) * (HDIM**-0.5)
-    scores = jnp.where(allowed, scores, FLOOR)
+    ) + bias
     peak = jnp.max(scores, axis=1, keepdims=True)
     weights = jnp.exp(scores - peak)
     total = jnp.sum(weights, axis=1, keepdims=True)
@@ -61,7 +60,7 @@
         count = jnp.sum(inside.astype(jnp.int32), axis=1, keepdims=True)
         hit = (position >= block * cap) & (position < block * cap + count)
         mask = mask | hit.astype(jnp.int32)
-    return mask
+    return jnp.where(mask > 0, 0.0, FLOOR)
 
 
 def kernel(
@@ -70,32 +69,32 @@
     tok,
     qi,
     ki,
-    lq,
-    lk,
-    lv,
-    lo,
-    hq,
-    hk,
-    hv,
-    ho,
-    out,
-    got_tok,
-    place_ref,
-    mask_ref,
-    pick,
-    pick_x,
-    pick_core,
-    light_q,
-    light_kv,
-    light_mix,
-    pairs,
-    queries,
-    mix,
-    walls,
-    placed,
-    send,
-    recv,
+    *refs,
 ):
+    far, out, near_refs = refs[:8], refs[8], refs[9:17]
+    lq, lk, lv, lo, hq, hk, hv, ho = near_refs
+    (
+        got_tok,
+        place_ref,
+        mask_ref,
+        pick,
+        pick_x,
+        pick_core,
+        light_q,
+        light_kv,
+        light_mix,
+        pairs,
+        queries,
+        mix,
+        walls,
+        placed,
+        load,
+        send,
+        recv,
+    ) = refs[17:]
+    loads = [
+        pltpu.make_async_copy(a, b, load.at[i]) for i, (a, b) in enumerate(zip(far, near_refs))
+    ]
     rows, width = tok.shape
     half = width // 2
     block_len = rows * group
@@ -143,6 +142,8 @@
     other = pl.multiple_of((1 - c) * half, half)
     tok_copy = remote(tok.at[:, pl.ds(other, half)], got_tok, core)
     tok_copy.start()
+    for i in (0, 1, 2, 5, 6, 4, 7, 3):
+        loads[i].start()
 
     first_token = s * block_len
     place_ref[:key_cap] = slot_places(ki, key_cap, first_token)
@@ -165,17 +166,19 @@
     span = pl.ds(0, key_cap)
     key_x = remote(pick.at[span], pick_x.at[span], xp)
     key_x.start()
-    wall_core = remote(ho, walls.at[0], core)
-    wall_core.start()
 
     spans = [(key_cap + i * TILE, TILE) for i in range(query_cap // TILE)]
     for start, size in spans:
         choose(start, size)
 
+    scale = jnp.asarray(HDIM**-0.5, jnp.bfloat16)
+    for i in (0, 1, 2):
+        loads[i].wait()
+
     def light_project(tile, carry):
         at = pl.multiple_of(tile * TILE, TILE)
         part = tok[pl.ds(at, TILE)]
-        light_q[pl.ds(at, TILE)] = dot16(part, lq[...])
+        light_q[pl.ds(at, TILE)] = (dot32(part, lq[...]).astype(jnp.bfloat16)) * scale
         light_kv[pl.ds(at + HALO, TILE), :lw] = dot16(part, lk[...])
         light_kv[pl.ds(at + HALO, TILE), lw:] = dot16(part, lv[...])
         return carry
@@ -189,41 +192,61 @@
     to_below.start()
 
     key_x.wait()
-    part_rows = ho.shape[0] // 2
-    wall_part = pl.ds(pl.multiple_of(y * part_rows, part_rows), part_rows)
-    wall_rest = pl.ds(pl.multiple_of((1 - y) * part_rows, part_rows), part_rows)
-    wall_x = remote(ho.at[wall_part], walls.at[1, wall_part], xp)
-    wall_x.start()
+    piece = ho.shape[0] // 4
+    ours = [pl.ds(pl.multiple_of((y * 2 + i) * piece, piece), piece) for i in range(2)]
+    theirs = [pl.ds(pl.multiple_of((2 - y * 2 + i) * piece, piece), piece) for i in range(2)]
 
     def join(start, size):
         rows_here = pl.ds(start, size)
-        pick[rows_here] = pick[rows_here] + pick_x[rows_here]
-        copy = remote(pick.at[rows_here], pick_core.at[rows_here], core)
+        pick_x[rows_here] = pick[rows_here] + pick_x[rows_here]
+        copy = remote(pick_x.at[rows_here], pick_core.at[rows_here], core)
         copy.start()
         return copy
 
     def project(start, size, matrix):
         return (
-            dot32(pick[start : start + size], matrix[pl.ds(mine, half)])
+            dot32(pick_x[start : start + size], matrix[pl.ds(mine, half)])
             + dot32(pick_core[start : start + size], matrix[pl.ds(other, half)])
         ).astype(jnp.bfloat16)
 
+    query_x = [
+        remote(pick.at[pl.ds(start, size)], pick_x.at[pl.ds(start, size)], xp)
+        for start, size in spans
+    ]
+    sent = [0]
+
+    def send_query():
+        if sent[0] < len(query_x):
+            if sent[0] >= 2:
+                query_x[sent[0] - 2].wait_send()
+            query_x[sent[0]].start()
+            sent[0] += 1
+
     key_core = join(0, key_cap)
-    query_x = []
-    for start, size in spans:
-        copy = remote(pick.at[pl.ds(start, size)], pick_x.at[pl.ds(start, size)], xp)
-        copy.start()
-        query_x.append(copy)
+    send_query()
+    send_query()
+    loads[5].wait()
+    loads[6].wait()
     key_core.wait_recv()
     pairs[s, :, :hw] = project(0, key_cap, hk)
     pairs[s, :, hw:] = project(0, key_cap, hv)
-    pair_z = [None]
-    for d in range(1, zs):
-        copy = remote(pairs.at[s], pairs.at[s], zp[d])
-        copy.start()
-        pair_z.append(copy)
+    order = sorted(range(1, zs), key=lambda d: min(d, zs - d))
+    pair_z = [remote(pairs.at[s], pairs.at[s], zp[d]) for d in order]
+    pair_z[0].start()
     pair_y = [remote(pairs.at[s], pairs.at[s], yp)]
     pair_y[0].start()
+    loads[7].wait()
+    wall_core = remote(ho, walls.at[0], core)
+    wall_core.start()
+
+    def forward_pair(number):
+        pair_z[number].wait()
+        if number + 1 < len(pair_z):
+            pair_z[number + 1].start()
+        slot = ((z + zs - order[number]) % zs) * 2 + y
+        copy = remote(pairs.at[slot], pairs.at[slot], yp)
+        copy.start()
+        pair_y.append(copy)
 
     to_above.wait_recv()
     to_below.wait_recv()
@@ -232,49 +255,69 @@
     k_off = lax.broadcasted_iota(jnp.int32, (HALO, reach), 1)
     near = jnp.abs(q_off - k_off) <= RADIUS
 
-    def light_tile(tile, carry):
-        at = pl.multiple_of(tile * HALO, HALO)
+    def light_tile(tile):
+        at = tile * HALO
         key_pos = flat * rows + (at - HALO) + k_off
         allowed = near & (key_pos >= 0) & (key_pos < total_len)
+        bias = jnp.where(allowed, 0.0, FLOOR)
         for head in range(lw // HDIM):
             lo_col, hi_col = head * HDIM, (head + 1) * HDIM
-            light_mix[pl.ds(at, HALO), lo_col:hi_col] = softmax_mix(
-                light_q[pl.ds(at, HALO), lo_col:hi_col],
-                light_kv[pl.ds(at, reach), lo_col:hi_col],
-                light_kv[pl.ds(at, reach), lw + lo_col : lw + hi_col],
-                allowed,
+            light_mix[at : at + HALO, lo_col:hi_col] = softmax_mix(
+                light_q[at : at + HALO, lo_col:hi_col],
+                light_kv[at : at + reach, lo_col:hi_col],
+                light_kv[at : at + reach, lw + lo_col : lw + hi_col],
+                bias,
             )
-        return carry
-
-    lax.fori_loop(0, rows // HALO, light_tile, 0)
-
-    for d in range(1, zs):
-        pair_z[d].wait_recv()
-        slot = ((z + zs - d) % zs) * 2 + y
-        copy = remote(pairs.at[slot], pairs.at[slot], yp)
+
+    tiles = rows // HALO
+    for tile in range(tiles):
+        light_tile(tile)
+        if tile == tiles // 2:
+            send_query()
+    forward_pair(0)
+    loads[4].wait()
+
+    query_core = []
+    for i in range(len(spans)):
+        query_x[i].wait_recv()
+        query_core.append(join(*spans[i]))
+        send_query()
+        if i + 1 < len(pair_z):
+            forward_pair(i + 1)
+        if i >= 1:
+            query_core[i - 1].wait_recv()
+            start, size = spans[i - 1]
+            queries[start - key_cap : start - key_cap + size] = (
+                project(start, size, hq) * scale
+            )
+    for number in range(len(spans) + 1, len(pair_z)):
+        forward_pair(number)
+    wall_x = [remote(ho.at[part], walls.at[1, part], xp) for part in ours]
+    for copy in wall_x:
         copy.start()
-        pair_y.append(copy)
-
-    wall_x.wait_recv()
-    wall_y = remote(walls.at[1, wall_part], walls.at[1, wall_part], yp)
-    wall_y.start()
-    wall_core_a = remote(walls.at[1, wall_part], walls.at[2, wall_part], core)
-    wall_core_a.start()
-
-    query_core = []
-    for i, (start, size) in enumerate(spans):
-        query_x[i].wait()
-        query_core.append(join(start, size))
+    query_core[-1].wait_recv()
+    start, size = spans[-1]
+    queries[start - key_cap : start - key_cap + size] = project(start, size, hq) * scale
     for copy in pair_y:
         copy.wait_recv()
+
+    wall_y, wall_far = [], []
+
+    def forward_wall():
+        number = len(wall_y)
+        if number < len(ours):
+            wall_x[number].wait_recv()
+            here = walls.at[1, ours[number]]
+            wall_y.append(remote(here, here, yp))
+            wall_y[-1].start()
+            wall_far.append(remote(here, walls.at[2, ours[number]], core))
+            wall_far[-1].start()
 
     keys = seq_count * key_cap
     step = TILE if keys <= 2048 else 32
     mix_x, mix_core, mix_far = [], [], []
     for i, (start, size) in enumerate(spans):
         at = start - key_cap
-        query_core[i].wait_recv()
-        queries[at : at + size] = project(start, size, hq)
 
         def heavy_tile(tile, carry):
             here = pl.multiple_of(at + tile * step, step)
@@ -284,7 +327,7 @@
                     queries[pl.ds(here, step), lo_col:hi_col],
                     pairs[:, :, lo_col:hi_col].reshape(keys, HDIM),
                     pairs[:, :, hw + lo_col : hw + hi_col].reshape(keys, HDIM),
-                    mask_ref[...] > 0,
+                    mask_ref[...],
                 )
             return carry
 
@@ -294,15 +337,15 @@
         mix_x[-1].start()
         mix_core.append(remote(mix.at[0, here], mix.at[1, here], core))
         mix_core[-1].start()
-        if i == 0:
-            wall_y.wait_recv()
-            wall_core_b = remote(walls.at[1, wall_rest], walls.at[2, wall_rest], core)
-            wall_core_b.start()
-        else:
+        if i >= 1:
             mix_x[i - 1].wait_recv()
             before = pl.ds(at - TILE, TILE)
             mix_far.append(remote(mix.at[2, before], mix.at[3, before], core))
             mix_far[-1].start()
+        if i >= len(spans) // 2 - 1:
+            forward_wall()
+    while len(wall_y) < len(ours):
+        forward_wall()
     mix_x[-1].wait_recv()
     last = pl.ds(query_cap - TILE, TILE)
     mix_far.append(remote(mix.at[2, last], mix.at[3, last], core))
@@ -323,8 +366,14 @@
         copy.wait_recv()
     back(3)
     wall_core.wait_recv()
-    wall_core_a.wait_recv()
-    wall_core_b.wait_recv()
+    for number, copy in enumerate(list(wall_y)):
+        copy.wait_recv()
+        here = walls.at[1, theirs[number]]
+        wall_far.append(remote(here, walls.at[2, theirs[number]], core))
+        wall_far[-1].start()
+    for copy in wall_far:
+        copy.wait_recv()
+    loads[3].wait()
 
     def finish(tile, carry):
         here = pl.ds(pl.multiple_of(tile * TILE, TILE), TILE)
@@ -339,7 +388,7 @@
 
     lax.fori_loop(0, rows // TILE, finish, 0)
 
-    waited = [key_x] + query_x
+    waited = [key_x] + query_x[: len(query_x) - 2] + pair_z
     for copy in begun:
         if not any(copy is done for done in waited):
             copy.wait_send()
@@ -357,12 +406,14 @@
     return pl.pallas_call(
         functools.partial(kernel, seq_count, group),
         out_shape=jax.ShapeDtypeStruct(tokens.shape, bf16),
-        in_specs=[pl.BlockSpec(memory_space=pltpu.VMEM)] * 11,
+        in_specs=[pl.BlockSpec(memory_space=pltpu.VMEM)] * 3
+        + [pl.BlockSpec(memory_space=pl.ANY)] * 8,
         out_specs=pl.BlockSpec(memory_space=pltpu.VMEM),
-        scratch_shapes=[
+        scratch_shapes=[pltpu.VMEM(weight.shape, bf16) for weight in weights]
+        + [
             pltpu.VMEM((rows, width // 2), bf16),
             pltpu.VMEM((slots, 1), jnp.int32),
-            pltpu.VMEM((1, seq_count * key_cap), jnp.int32),
+            pltpu.VMEM((1, seq_count * key_cap), jnp.float32),
             pltpu.VMEM((slots, width // 2), bf16),
             pltpu.VMEM((slots, width // 2), bf16),
             pltpu.VMEM((slots, width // 2), bf16),
@@ -374,6 +425,7 @@
             pltpu.VMEM((4, query_cap, hw), bf16),
             pltpu.VMEM((3,) + weights[7].shape, bf16),
             pltpu.VMEM((4, rows, hw), bf16),
+            pltpu.SemaphoreType.DMA((8,)),
             pltpu.SemaphoreType.DMA((copies,)),
             pltpu.SemaphoreType.DMA((copies,)),
         ],

time: 86.1 us -> 85.3 us (level)
  Pallas kernels: 82.2 us -> 80.6 us
    pallas_call x1, Pallas kernels: 82.2 us -> 80.6 us  [shards(): pl.pallas_call(functools.partial(kernel, seq_count, group), out_shape=jax...]
where the time goes in v3:
time: 85.3 us; the launch traced here: 83.7 us
  Pallas kernels  80.6 us (94%)
  local copies, waits for them, and re-layouts  3.16 us (4%)
    pallas_call x1, Pallas kernels, shards(): pl.pallas_call(functools.partial(kernel, seq_count, group), out_shape=jax...  80.6 us
    unnamed x1, local copies, waits for them, and re-layouts  3.16 us

profile of v3, /device:TPU:0, one launch (start us, length us, event | category | flops | bytes accessed | tf_op | source)
XLA Modules:
  0.0 83.7 jit_solution(13051714149533499709)
XLA Ops:
  0.0 80.6 %shard_map.109 = bf16[512,2048]{1,0:T(8,128)(2,1)} custom-call(bf16[512,2048]{1,0:T(8,128)(2,1)} %tok.1, s32[1,1024]{1,0:T(1,128)} %bitcast.2, s32[1,1024]{1,0:T(1,128)} %bitcast.3, bf16[2048,256]{1,0:T(8,128)(2,1)} %refs_0_.1, bf16[2048,256]{1,0:T(8,128)(2,1)} %refs_1_.1, bf16[2048,256]{1,0:T(8,128)(2,1)} %refs_2_.1, bf16[256,2048]{1,0:T(8,128)(2,1)} %refs_3_.1, ...), custom_call_target="tpu_custom_call" | custom-call | tf_op jit(solution)/shard_map/pallas_call | solution.py:406
  80.6 3.2 %copy.13 = bf16[512,2048]{1,0:T(8,128)(2,1)} copy(bf16[512,2048]{1,0:T(8,128)(2,1)} %shard_map.109) | data formatting | bytes 4194304

commit v4 on v3

--- a/solution.py
+++ b/solution.py
@@ -142,6 +142,14 @@
     other = pl.multiple_of((1 - c) * half, half)
     tok_copy = remote(tok.at[:, pl.ds(other, half)], got_tok, core)
     tok_copy.start()
+    zl = z % 2
+    zmate = ((z + 1 - 2 * zl) * 2 + y, h)
+    piece = ho.shape[0] // 4
+    first_piece = pl.ds(pl.multiple_of((zl * 2 + y) * piece, piece), piece)
+    first_half = pl.ds(pl.multiple_of(zl * 2 * piece, 2 * piece), 2 * piece)
+    rest_half = pl.ds(pl.multiple_of((1 - zl) * 2 * piece, 2 * piece), 2 * piece)
+    wall_x = remote(far[7].at[first_piece], walls.at[1, first_piece], xp)
+    wall_x.start()
     for i in (0, 1, 2, 5, 6, 4, 7, 3):
         loads[i].start()
 
@@ -192,9 +200,9 @@
     to_below.start()
 
     key_x.wait()
-    piece = ho.shape[0] // 4
-    ours = [pl.ds(pl.multiple_of((y * 2 + i) * piece, piece), piece) for i in range(2)]
-    theirs = [pl.ds(pl.multiple_of((2 - y * 2 + i) * piece, piece), piece) for i in range(2)]
+    wall_x.wait_recv()
+    wall_y = remote(walls.at[1, first_piece], walls.at[1, first_piece], yp)
+    wall_y.start()
 
     def join(start, size):
         rows_here = pl.ds(start, size)
@@ -238,6 +246,9 @@
     loads[7].wait()
     wall_core = remote(ho, walls.at[0], core)
     wall_core.start()
+    wall_y.wait_recv()
+    wall_far_a = remote(walls.at[1, first_half], walls.at[2, first_half], core)
+    wall_far_a.start()
 
     def forward_pair(number):
         pair_z[number].wait()
@@ -292,26 +303,13 @@
             )
     for number in range(len(spans) + 1, len(pair_z)):
         forward_pair(number)
-    wall_x = [remote(ho.at[part], walls.at[1, part], xp) for part in ours]
-    for copy in wall_x:
-        copy.start()
+    wall_z = remote(walls.at[1, first_half], walls.at[1, first_half], zmate)
+    wall_z.start()
     query_core[-1].wait_recv()
     start, size = spans[-1]
     queries[start - key_cap : start - key_cap + size] = project(start, size, hq) * scale
     for copy in pair_y:
         copy.wait_recv()
-
-    wall_y, wall_far = [], []
-
-    def forward_wall():
-        number = len(wall_y)
-        if number < len(ours):
-            wall_x[number].wait_recv()
-            here = walls.at[1, ours[number]]
-            wall_y.append(remote(here, here, yp))
-            wall_y[-1].start()
-            wall_far.append(remote(here, walls.at[2, ours[number]], core))
-            wall_far[-1].start()
 
     keys = seq_count * key_cap
     step = TILE if keys <= 2048 else 32
@@ -342,10 +340,6 @@
             before = pl.ds(at - TILE, TILE)
             mix_far.append(remote(mix.at[2, before], mix.at[3, before], core))
             mix_far[-1].start()
-        if i >= len(spans) // 2 - 1:
-            forward_wall()
-    while len(wall_y) < len(ours):
-        forward_wall()
     mix_x[-1].wait_recv()
     last = pl.ds(query_cap - TILE, TILE)
     mix_far.append(remote(mix.at[2, last], mix.at[3, last], core))
@@ -366,13 +360,11 @@
         copy.wait_recv()
     back(3)
     wall_core.wait_recv()
-    for number, copy in enumerate(list(wall_y)):
-        copy.wait_recv()
-        here = walls.at[1, theirs[number]]
-        wall_far.append(remote(here, walls.at[2, theirs[number]], core))
-        wall_far[-1].start()
-    for copy in wall_far:
-        copy.wait_recv()
+    wall_far_a.wait_recv()
+    wall_z.wait_recv()
+    wall_far_b = remote(walls.at[1, rest_half], walls.at[2, rest_half], core)
+    wall_far_b.start()
+    wall_far_b.wait_recv()
     loads[3].wait()
 
     def finish(tile, carry):

time: 85.3 us -> 80.4 us (0.943); the launches traced: 83.7 us -> 79.9 us
  Pallas kernels: 80.6 us -> 76.7 us
    pallas_call x1, Pallas kernels: 80.6 us -> 76.7 us  [shards(): pl.pallas_call(functools.partial(kernel, seq_count, group), out_shape=jax...]
where the time goes in v4:
time: 80.4 us; the launch traced here: 79.9 us
  Pallas kernels  76.7 us (95%)
  local copies, waits for them, and re-layouts  3.16 us (4%)
    pallas_call x1, Pallas kernels, shards(): pl.pallas_call(functools.partial(kernel, seq_count, group), out_shape=jax...  76.7 us
    unnamed x1, local copies, waits for them, and re-layouts  3.16 us

profile of v4, /device:TPU:0, one launch (start us, length us, event | category | flops | bytes accessed | tf_op | source)
XLA Modules:
  0.0 79.9 jit_solution(6077621861220338469)
XLA Ops:
  0.0 76.7 %shard_map.109 = bf16[512,2048]{1,0:T(8,128)(2,1)} custom-call(bf16[512,2048]{1,0:T(8,128)(2,1)} %tok.1, s32[1,1024]{1,0:T(1,128)} %bitcast.2, s32[1,1024]{1,0:T(1,128)} %bitcast.3, bf16[2048,256]{1,0:T(8,128)(2,1)} %refs_0_.1, bf16[2048,256]{1,0:T(8,128)(2,1)} %refs_1_.1, bf16[2048,256]{1,0:T(8,128)(2,1)} %refs_2_.1, bf16[256,2048]{1,0:T(8,128)(2,1)} %refs_3_.1, ...), custom_call_target="tpu_custom_call" | custom-call | tf_op jit(solution)/shard_map/pallas_call | solution.py:398
  76.8 3.2 %copy.13 = bf16[512,2048]{1,0:T(8,128)(2,1)} copy(bf16[512,2048]{1,0:T(8,128)(2,1)} %shard_map.109) | data formatting | bytes 4194304

commit v5 on v4

--- a/solution.py
+++ b/solution.py
@@ -88,6 +88,7 @@
         mix,
         walls,
         placed,
+        back_ref,
         load,
         send,
         recv,
@@ -289,7 +290,7 @@
     loads[4].wait()
 
     query_core = []
-    for i in range(len(spans)):
+    for i in range(len(spans) - 1):
         query_x[i].wait_recv()
         query_core.append(join(*spans[i]))
         send_query()
@@ -301,13 +302,22 @@
             queries[start - key_cap : start - key_cap + size] = (
                 project(start, size, hq) * scale
             )
-    for number in range(len(spans) + 1, len(pair_z)):
+    for number in range(len(spans), len(pair_z)):
         forward_pair(number)
     wall_z = remote(walls.at[1, first_half], walls.at[1, first_half], zmate)
     wall_z.start()
-    query_core[-1].wait_recv()
-    start, size = spans[-1]
-    queries[start - key_cap : start - key_cap + size] = project(start, size, hq) * scale
+    while sent[0] < len(query_x):
+        send_query()
+
+    def settle(i):
+        query_core[i].wait_recv()
+        start, size = spans[i]
+        queries[start - key_cap : start - key_cap + size] = project(start, size, hq) * scale
+
+    settle(len(spans) - 2)
+    back_ref[...] = (
+        chosen(key_cap, query_cap, h).astype(jnp.float32).T.astype(jnp.bfloat16)
+    )
     for copy in pair_y:
         copy.wait_recv()
 
@@ -316,6 +326,11 @@
     mix_x, mix_core, mix_far = [], [], []
     for i, (start, size) in enumerate(spans):
         at = start - key_cap
+        if i == len(spans) - 2:
+            query_x[-1].wait_recv()
+            query_core.append(join(*spans[-1]))
+        if i == len(spans) - 1:
+            settle(i)
 
         def heavy_tile(tile, carry):
             here = pl.multiple_of(at + tile * step, step)
@@ -345,11 +360,13 @@
     mix_far.append(remote(mix.at[2, last], mix.at[3, last], core))
     mix_far[-1].start()
 
+    wall_far_a.wait_recv()
+    wall_z.wait_recv()
+    wall_far_b = remote(walls.at[1, rest_half], walls.at[2, rest_half], core)
+    wall_far_b.start()
+
     def back(part):
-        pick_t = chosen(key_cap, query_cap, h)
-        placed[part] = lax.dot_general(
-            pick_t, mix[part], (((0,), (0,)), ((), ())), preferred_element_type=jnp.float32
-        ).astype(jnp.bfloat16)
+        placed[part] = dot16(back_ref[...], mix[part])
 
     back(0)
     for copy in mix_core:
@@ -360,10 +377,6 @@
         copy.wait_recv()
     back(3)
     wall_core.wait_recv()
-    wall_far_a.wait_recv()
-    wall_z.wait_recv()
-    wall_far_b = remote(walls.at[1, rest_half], walls.at[2, rest_half], core)
-    wall_far_b.start()
     wall_far_b.wait_recv()
     loads[3].wait()
 
@@ -417,6 +430,7 @@
             pltpu.VMEM((4, query_cap, hw), bf16),
             pltpu.VMEM((3,) + weights[7].shape, bf16),
             pltpu.VMEM((4, rows, hw), bf16),
+            pltpu.VMEM((rows, query_cap), bf16),
             pltpu.SemaphoreType.DMA((8,)),
             pltpu.SemaphoreType.DMA((copies,)),
             pltpu.SemaphoreType.DMA((copies,)),

time: 80.4 us -> 79.3 us (0.986)
  Pallas kernels: 76.7 us -> 75.7 us
    pallas_call x1, Pallas kernels: 76.7 us -> 75.7 us  [shards(): pl.pallas_call(functools.partial(kernel, seq_count, group), out_shape=jax...]
where the time goes in v5:
time: 79.3 us; the launch traced here: 78.9 us
  Pallas kernels  75.7 us (95%)
  local copies, waits for them, and re-layouts  3.16 us (4%)
    pallas_call x1, Pallas kernels, shards(): pl.pallas_call(functools.partial(kernel, seq_count, group), out_shape=jax...  75.7 us
    unnamed x1, local copies, waits for them, and re-layouts  3.16 us

profile of v5, /device:TPU:0, one launch (start us, length us, event | category | flops | bytes accessed | tf_op | source)
XLA Modules:
  0.0 78.9 jit_solution(456513228319219082)
XLA Ops:
  0.0 75.7 %shard_map.109 = bf16[512,2048]{1,0:T(8,128)(2,1)} custom-call(bf16[512,2048]{1,0:T(8,128)(2,1)} %tok.1, s32[1,1024]{1,0:T(1,128)} %bitcast.2, s32[1,1024]{1,0:T(1,128)} %bitcast.3, bf16[2048,256]{1,0:T(8,128)(2,1)} %refs_0_.1, bf16[2048,256]{1,0:T(8,128)(2,1)} %refs_1_.1, bf16[2048,256]{1,0:T(8,128)(2,1)} %refs_2_.1, bf16[256,2048]{1,0:T(8,128)(2,1)} %refs_3_.1, ...), custom_call_target="tpu_custom_call" | custom-call | tf_op jit(solution)/shard_map/pallas_call | solution.py:411
  75.7 3.2 %copy.13 = bf16[512,2048]{1,0:T(8,128)(2,1)} copy(bf16[512,2048]{1,0:T(8,128)(2,1)} %shard_map.109) | data formatting | bytes 4194304
